TPU v7x, 32 devices: a whole 2x2x4 slice. The times are simulated.
32 devices in a mesh: groups: 2 (over y), gy: 4 (over z), gz: 2 (over x), gx: 2 (over core).
Axes of the slice: x: 2, y: 2, z: 4, core: 2. Of those that a mesh axis runs over, the one named last changes fastest.
Arguments:
- block_input: bfloat16 [12, 4, 72, 768], P(None, 'gz', ('groups', 'gy'), 'gx'), parts along dimension 2, may hold values from -6 to 6
- first_pre: bfloat16 [12, 4, 72, 768], P(None, 'gz', ('groups', 'gy'), 'gx'), parts along dimension 2, may hold values from -6 to 6
- second_pre: bfloat16 [60, 4, 24, 256], P(None, 'gz', ('groups', 'gy'), 'gx'), parts along dimension 2, may hold values from -6 to 6
- output_cotangent: bfloat16 [60, 4, 24, 256], P(None, 'gz', ('groups', 'gy'), 'gx'), parts along dimension 2, may hold values from -6 to 6
- first_kernel: bfloat16 [3, 3, 3, 12, 12], replicated, may hold values from -0.3125 to 0.3125
- second_kernel: bfloat16 [3, 3, 60, 12], replicated, may hold values from -0.625 to 0.625
- third_kernel: bfloat16 [3, 3, 60, 60], replicated, may hold values from -0.25 to 0.25
Outputs:
- block_gradient: bfloat16 [12, 4, 72, 768], P(None, 'gz', ('groups', 'gy'), 'gx'), parts along dimension 2
- first_gradient: float32 [6, 3, 3, 12, 12], P('groups'), parts along dimension 0
- second_gradient: float32 [6, 3, 60, 12], P('groups'), parts along dimension 0
- third_gradient: float32 [6, 3, 60, 60], P('groups'), parts along dimension 0
There are 2 independent parts, one for each index of `groups`. A program takes and returns all parts, laid end to end along the dimension named above; an argument that names none is the same for every part. Nothing has to cross between parts.
All inputs are finite; a program needn't handle non-finite values.
Results may differ from a plain program's by a relative error of at most 0.0057.
Values may be sent and summed in bfloat16 or wider, within the bound.
A program may use at most 64 MiB of HBM per device.

v0:
```python
import functools
import math

import jax
import jax.numpy as jnp
import numpy as np
from jax import lax
from jax.experimental import pallas as pl
from jax.experimental.pallas import tpu as pltpu
from jax.sharding import PartitionSpec as P

MESH = pl.DeviceIdType.MESH
F32, BF16 = jnp.float32, jnp.bfloat16


def dot(a, b, da, db):
    return lax.dot_general(a, b, (((da,), (db,)), ((), ())), preferred_element_type=F32)


def neighbour_moves(sections):
    return [(z, y, s) for z in sections for y in (-1, 0, 1) for s in (0, 1) if (z, y, s) != (0, 0, 0)]


COARSE = neighbour_moves((0,))
FINE = neighbour_moves((-1, 0, 1))


def kernel(
    ny, nz, rows,
    bi_ref, fp_ref, sp_ref, oc_ref, w1_ref, w2_ref, w3_ref, pick_ref, back_ref,
    out_ref, total_ref,
    cot, delta, fine, col, ext, split, lanes, gather, grad, inbox,
    cot_s, cot_r, delta_s, delta_r, fine_s, fine_r, sum_s, sum_r, all_s, all_r,
):
    gy, gz, gx = lax.axis_index("gy"), lax.axis_index("gz"), lax.axis_index("gx")

    def there(z, y):
        ok = None
        for at, step, size in ((gz, z, nz), (gy, y, ny)):
            if step:
                one = at < size - 1 if step > 0 else at > 0
                ok = one if ok is None else jnp.logical_and(ok, one)
        return ok

    def guarded(z, y, run):
        ok = there(z, y)
        if ok is None:
            run()
        else:
            pl.when(ok)(run)

    def device(z, y, s):
        return {"gz": gz + z, "gy": gy + y, "gx": 1 - gx if s else gx}

    cot[...] = jnp.zeros_like(cot)
    delta[...] = jnp.zeros_like(delta)
    fine[...] = jnp.zeros_like(fine)
    for z in range(2):
        for y in range(3):
            cot[0, z, y + 1] = oc_ref[z, y]

    barrier = pltpu.get_barrier_semaphore()
    count = jnp.int32(0)
    for z, y, s in FINE:
        def greet(z=z, y=y, s=s):
            pl.semaphore_signal(barrier, inc=1, device_id=device(z, y, s), device_id_type=MESH)
        guarded(z, y, greet)
        ok = there(z, y)
        count = count + (1 if ok is None else ok.astype(jnp.int32))
    for j in range(1, nz):
        pl.semaphore_signal(barrier, inc=1, device_id={"gz": lax.rem(gz + j, nz)}, device_id_type=MESH)
    for j in range(1, ny):
        pl.semaphore_signal(barrier, inc=1, device_id={"gy": lax.rem(gy + j, ny)}, device_id_type=MESH)
    pl.semaphore_wait(barrier, count + (nz - 1) + (ny - 1))

    def halo_copy(buf, send, recv, moves, m, arriving=False):
        z, y, s = moves[m]
        zs = slice(0, 2) if buf.shape[1] == 2 else slice(1, 3)
        zd = zs
        if z:
            zs, zd = (slice(2, 3), slice(0, 1)) if z > 0 else (slice(1, 2), slice(3, 4))
        ys = yd = slice(1, 4)
        if y:
            ys, yd = (slice(3, 4), slice(0, 1)) if y > 0 else (slice(1, 2), slice(4, 5))
        return pltpu.make_async_remote_copy(
            src_ref=buf.at[0, zs, ys], dst_ref=buf.at[s, zd, yd],
            send_sem=send.at[m], recv_sem=recv.at[m],
            device_id=device(z, y, s), device_id_type=MESH,
        )

    def start_halo(buf, send, recv, moves):
        for m, (z, y, s) in enumerate(moves):
            guarded(z, y, lambda m=m: halo_copy(buf, send, recv, moves, m).start())

    def wait_halo(buf, send, recv, moves):
        for m, (z, y, s) in enumerate(moves):
            guarded(-z, -y, lambda m=m: halo_copy(buf, send, recv, moves, m).wait_recv())

    def wait_sent(buf, send, recv, moves):
        for m, (z, y, s) in enumerate(moves):
            guarded(z, y, lambda m=m: halo_copy(buf, send, recv, moves, m).wait_send())

    def shifted(own, other):
        own, other = own.astype(F32), other.astype(F32)
        lane = lax.broadcasted_iota(jnp.int32, own.shape, 1)
        left = jnp.where(gx == 1, other, 0.0)
        right = jnp.where(gx == 0, other, 0.0)
        before = pltpu.roll(jnp.where(lane == 127, left, own), 1, 1)
        after = pltpu.roll(jnp.where(lane == 0, right, own), 127, 1)
        return before, after

    def columns(buf):
        for z in range(2):
            for y in range(5):
                own = buf[0, z, y]
                before, after = shifted(own, buf[1, z, y])
                for ex, slab in enumerate((before.astype(BF16), own, after.astype(BF16))):
                    for ey in range(3):
                        yc = y - ey
                        if 0 <= yc < 3:
                            r = (ey * 3 + ex) * 64
                            c = (z * 3 + yc) * 128
                            col[r:r + 64, c:c + 128] = slab

    start_halo(cot, cot_s, cot_r, COARSE)

    split[...] = dot(fp_ref[...], pick_ref[...], 1, 0)

    def phase(z, a, b):
        return jnp.concatenate(
            [split[(z * 9 + 3 * yc + a) * 16:(z * 9 + 3 * yc + a) * 16 + 16, b * 128:b * 128 + 128] for yc in range(3)],
            axis=1,
        )

    pooled = []
    for z in range(2):
        window = [jnp.maximum(phase(z, k // 3, k % 3), 0.0) for k in range(9)]
        top = functools.reduce(jnp.maximum, window)
        first = jnp.full(top.shape, 9.0, F32)
        for k in reversed(range(9)):
            first = jnp.where(window[k] == top, float(k), first)
        first = jnp.where(top > 0.0, first, 9.0).astype(BF16)
        for y in range(3):
            fine[0, z + 1, y + 1, 16:32] = first[:, y * 128:y * 128 + 128]
        pooled.append(top.astype(BF16))
    lanes[...] = jnp.zeros_like(lanes)
    for z in range(2):
        for y in range(3):
            c = (z * 3 + y) * 128
            lanes[0, 0:64, c:c + 128] = jnp.maximum(sp_ref[z, y], jnp.zeros((), BF16))
        lanes[1, 64:80, z * 384:z * 384 + 384] = pooled[z]
    split[...] = dot(bi_ref[...], pick_ref[...], 1, 0)

    wait_halo(cot, cot_s, cot_r, COARSE)
    columns(cot)
    third_back = dot(w3_ref[...], col[...], 0, 0)
    for z in range(2):
        for y in range(3):
            c = (z * 3 + y) * 128
            delta[0, z, y + 1] = jnp.where(
                sp_ref[z, y].astype(F32) > 0.0, third_back[:, c:c + 128], 0.0
            ).astype(BF16)
    start_halo(delta, delta_s, delta_r, COARSE)
    grad[...] = jnp.zeros_like(grad)
    grad[0:576] = dot(col[...], lanes[0], 1, 1)
    wait_halo(delta, delta_s, delta_r, COARSE)
    columns(delta)
    pooled_back = dot(w2_ref[...], col[...], 0, 0).astype(BF16)
    for z in range(2):
        for y in range(3):
            c = (z * 3 + y) * 128
            fine[0, z + 1, y + 1, 0:16] = pooled_back[:, c:c + 128]
    start_halo(fine, fine_s, fine_r, FINE)
    grad[0:576] += dot(col[...], lanes[1], 1, 1)
    wait_halo(fine, fine_s, fine_r, FINE)

    for z in range(4):
        own = fine[0, z].reshape(160, 128)
        before, after = shifted(own, fine[1, z].reshape(160, 128))
        own = own.astype(F32)
        views = []
        for src in (before, own, after):
            value = [src[y * 32:y * 32 + 16] for y in range(5)]
            place = [src[y * 32 + 16:y * 32 + 32] for y in range(5)]
            views.append((value, place))
        for ea in range(5):
            a, up = ((2, 0), (0, 1), (1, 1), (2, 1), (0, 2))[ea]
            for eb in range(5):
                b, side = ((2, 0), (0, 1), (1, 1), (2, 1), (0, 2))[eb]
                value, place = views[side]
                for yc in range(3):
                    block = jnp.where(place[yc + up] == float(a * 3 + b), value[yc + up], 0.0)
                    r = (ea * 5 + eb) * 16
                    ext[z, r:r + 16, yc * 128:yc * 128 + 128] = block.astype(BF16)

    first = jnp.zeros((16, 432), F32)
    for z in range(2):
        for a in range(3):
            for b in range(3):
                stack = jnp.concatenate(
                    [
                        ext[z + ez, ((a + ey) * 5 + b) * 16:((a + ey) * 5 + b) * 16 + 48]
                        for ez in range(3) for ey in range(3)
                    ],
                    axis=0,
                )
                back = dot(w1_ref[...], stack, 0, 0).astype(BF16)
                for yc in range(3):
                    r = (z * 9 + 3 * yc + a) * 16
                    gather[r:r + 16, b * 128:b * 128 + 128] = back[:, yc * 128:yc * 128 + 128]
                first = first + dot(phase(z, a, b).astype(BF16), stack, 1, 1)
    for k in range(3):
        grad[576 + k * 16:592 + k * 16] = first[:, k * 128:k * 128 + 128]
    grad[624:640, 0:48] = first[:, 384:432]

    stages = (("gx", gx, 2), ("gz", gz, nz), ("gy", gy, ny))
    offset, length, slot = jnp.int32(0), rows, 0
    done = []
    sends = []
    for axis, at, size in stages:
        share = length // size
        mine = pl.multiple_of(offset + at * share, 8)
        copies = []
        for j in range(1, size):
            peer = lax.rem(at + j, size)
            copy = pltpu.make_async_remote_copy(
                src_ref=grad.at[pl.ds(pl.multiple_of(offset + peer * share, 8), share)],
                dst_ref=inbox.at[slot + j - 1, pl.ds(0, share)],
                send_sem=sum_s.at[slot + j - 1], recv_sem=sum_r.at[slot + j - 1],
                device_id={axis: peer}, device_id_type=MESH,
            )
            copy.start()
            copies.append(copy)
        if axis == "gx":
            result = dot(gather[...], back_ref[...], 1, 0)
            out_ref[...] = result.astype(BF16)
        for copy in copies:
            copy.wait_recv()
        total = grad[pl.ds(mine, share)]
        for j in range(1, size):
            total = total + inbox[slot + j - 1, 0:share]
        grad[pl.ds(mine, share)] = total
        sends += copies
        done.append((axis, at, size, slot))
        slot += size - 1
        offset, length = mine, share
    total_ref[pl.ds(offset, length)] = grad[pl.ds(offset, length)]
    for axis, at, size, slot in reversed(done):
        copies = []
        for j in range(1, size):
            peer = lax.rem(at + j, size)
            copy = pltpu.make_async_remote_copy(
                src_ref=total_ref.at[pl.ds(offset, length)],
                dst_ref=total_ref.at[pl.ds(offset, length)],
                send_sem=all_s.at[slot + j - 1], recv_sem=all_r.at[slot + j - 1],
                device_id={axis: peer}, device_id_type=MESH,
            )
            copy.start()
            copies.append(copy)
        for copy in copies:
            copy.wait_recv()
        sends += copies
        offset = pl.multiple_of(offset - at * length, 8)
        length = length * size
    for copy in sends:
        copy.wait_send()
    wait_sent(cot, cot_s, cot_r, COARSE)
    wait_sent(delta, delta_s, delta_r, COARSE)
    wait_sent(fine, fine_s, fine_r, FINE)


def on_device(
    block_input, first_pre, second_pre, output_cotangent, first_kernel, second_kernel, third_kernel
):
    ny, nz, nx = (lax.axis_size(axis) for axis in ("gy", "gz", "gx"))
    assert nx == 2 and block_input.shape == (12, 2, 9, 384)
    devices = ny * nz * nx
    rows = devices * (-(-640 // (devices * 8)) * 8)

    def fine_rows(x):
        return jnp.pad(x.transpose(1, 2, 0, 3), ((0, 0), (0, 0), (0, 4), (0, 0))).reshape(288, 384)

    def coarse_rows(x):
        return jnp.pad(x.transpose(1, 2, 0, 3), ((0, 0), (0, 0), (0, 4), (0, 0)))

    w1 = jnp.pad(jnp.flip(first_kernel, (0, 1, 2)), ((0, 0),) * 3 + ((0, 4), (0, 4))).reshape(432, 16)
    w2 = jnp.pad(jnp.flip(second_kernel, (0, 1)), ((0, 0),) * 2 + ((0, 4), (0, 4))).reshape(576, 16)
    w3 = jnp.pad(jnp.flip(third_kernel, (0, 1)), ((0, 0),) * 2 + ((0, 4), (0, 4))).reshape(576, 64)
    pick = np.zeros((384, 384), np.float32)
    x = np.arange(384)
    pick[x, (x % 3) * 128 + x // 3] = 1.0
    slots = 1 + (nz - 1) + (ny - 1)
    dma = pltpu.SemaphoreType.DMA
    vmem = pl.BlockSpec(memory_space=pltpu.VMEM)
    out, total = pl.pallas_call(
        functools.partial(kernel, ny, nz, rows),
        out_shape=(
            jax.ShapeDtypeStruct((288, 384), BF16),
            jax.ShapeDtypeStruct((rows, 128), F32),
        ),
        in_specs=[vmem] * 9,
        out_specs=(vmem, vmem),
        scratch_shapes=[
            pltpu.VMEM((2, 2, 5, 64, 128), BF16),
            pltpu.VMEM((2, 2, 5, 64, 128), BF16),
            pltpu.VMEM((2, 4, 5, 32, 128), BF16),
            pltpu.VMEM((576, 768), BF16),
            pltpu.VMEM((4, 400, 384), BF16),
            pltpu.VMEM((288, 384), F32),
            pltpu.VMEM((2, 128, 768), BF16),
            pltpu.VMEM((288, 384), BF16),
            pltpu.VMEM((rows, 128), F32),
            pltpu.VMEM((slots, rows // 2, 128), F32),
            dma((len(COARSE),)), dma((len(COARSE),)),
            dma((len(COARSE),)), dma((len(COARSE),)),
            dma((len(FINE),)), dma((len(FINE),)),
            dma((slots,)), dma((slots,)), dma((slots,)), dma((slots,)),
        ],
        compiler_params=pltpu.CompilerParams(
            collective_id=0, has_side_effects=True, vmem_limit_bytes=48 * 1024 * 1024
        ),
    )(
        fine_rows(block_input), fine_rows(first_pre), coarse_rows(second_pre), coarse_rows(output_cotangent),
        w1, w2, w3, jnp.asarray(pick, BF16), jnp.asarray(pick.T, BF16),
    )
    block_gradient = out.reshape(2, 9, 16, 384)[:, :, :12].transpose(2, 0, 1, 3)
    voxels = 2 * 9 * 384 * devices
    coarse_scale = math.sqrt(voxels // 9)
    fine_scale = math.sqrt(voxels)
    third = jnp.flip(total[:576, :64].reshape(3, 3, 64, 64)[:, :, :60, :60], (0, 1))
    second = jnp.flip(total[:576, 64:80].reshape(3, 3, 64, 16)[:, :, :60, :12], (0, 1))
    first = total[576:640].reshape(4, 16, 128).transpose(0, 2, 1).reshape(512, 16)[:432]
    first = jnp.flip(first.reshape(3, 3, 3, 16, 16)[..., :12, :12], (0, 1, 2))
    return block_gradient, first / fine_scale, second / coarse_scale, third / coarse_scale


def solution(mesh):
    volume = P(None, "gz", ("groups", "gy"), "gx")
    return jax.shard_map(
        on_device,
        mesh=mesh,
        in_specs=(volume,) * 4 + (P(),) * 3,
        out_specs=(
            volume,
            P("groups", None, None, None, None),
            P("groups", None, None, None),
            P("groups", None, None, None),
        ),
        check_vma=False,
    )
```

profile of v0, /device:TPU:0, one launch (start us, length us, event | category | flops | bytes accessed | tf_op | source)
XLA Modules:
  0.0 49.7 jit_solution(18156586757919065128)
XLA Ops:
  0.6 0.8 %rev.25 = bf16[3,3,60,12]{2,3,1,0:T(8,128)(2,1)S(1)} reverse(bf16[3,3,60,12]{2,3,1,0:T(8,128)(2,1)} %param.14), dimensions={0,1} | reverse | bytes 25920 | tf_op jit(solution)/shard_map/jit(_flip)/rev | solution.py:287
  1.4 0.9 %copy.50 = bf16[60,2,3,128]{3,0,2,1:T(8,128)(2,1)S(1)} copy(bf16[60,2,3,128]{3,1,2,0:T(2,128)(2,1)} %param.11) | data formatting | bytes 184320 | tf_op args[2]
  2.3 0.0 copy-start.6
  2.3 0.9 %copy-done.6 = bf16[60,2,3,128]{3,1,2,0:T(2,128)(2,1)S(1)} copy-done((bf16[60,2,3,128]{3,1,2,0:T(2,128)(2,1)S(1)}, bf16[60,2,3,128]{3,1,2,0:T(2,128)(2,1)}, u32[]{:S(2)}) %copy-start.6) | copy-done | bytes 92184
  3.2 0.2 copy.42
  3.4 0.0 copy-start.5
  3.5 0.9 %copy-done.5 = bf16[3,3,3,12,12]{4,3,2,1,0:T(8,128)(2,1)S(1)} copy-done((bf16[3,3,3,12,12]{4,3,2,1,0:T(8,128)(2,1)S(1)}, bf16[3,3,3,12,12]{4,3,2,1,0:T(8,128)(2,1)}, u32[]{:S(2)}) %copy-start.5) | copy-done | bytes 7800
  4.3 0.0 copy-start.4
  4.4 0.9 %copy-done.4 = bf16[3,3,60,60]{3,2,1,0:T(8,128)(2,1)S(1)} copy-done((bf16[3,3,60,60]{3,2,1,0:T(8,128)(2,1)S(1)}, bf16[3,3,60,60]{3,2,1,0:T(8,128)(2,1)}, u32[]{:S(2)}) %copy-start.4) | copy-done | bytes 64824
  5.3 0.0 copy-start.2
  5.3 0.9 %copy-done.2 = bf16[12,2,9,384]{3,1,2,0:T(2,128)(2,1)S(1)} copy-done((bf16[12,2,9,384]{3,1,2,0:T(2,128)(2,1)S(1)}, bf16[12,2,9,384]{3,1,2,0:T(2,128)(2,1)}, u32[]{:S(2)}) %copy-start.2) | copy-done | bytes 165912
  6.2 0.0 copy-start.3
  6.3 0.9 %copy-done.3 = bf16[12,2,9,384]{3,1,2,0:T(2,128)(2,1)S(1)} copy-done((bf16[12,2,9,384]{3,1,2,0:T(2,128)(2,1)S(1)}, bf16[12,2,9,384]{3,1,2,0:T(2,128)(2,1)}, u32[]{:S(2)}) %copy-start.3) | copy-done | bytes 165912
  7.1 0.0 copy-start.1
  7.2 0.0 copy-start
  7.2 0.9 %copy-done.1 = bf16[384,384]{1,0:T(8,128)(2,1)S(1)} copy-done((bf16[384,384]{1,0:T(8,128)(2,1)S(1)}, bf16[384,384]{1,0:T(8,128)(2,1)}, u32[]{:S(2)}) %copy-start.1) | copy-done | bytes 294936
  8.1 0.1 copy-done
  8.2 37.4 %shard_map.120 = (bf16[288,384]{1,0:T(8,128)(2,1)S(1)}, f32[640,128]{1,0:T(8,128)S(1)}) custom-call(bf16[288,384]{1,0:T(8,128)(2,1)S(1)} %bitcast.33, bf16[288,384]{1,0:T(8,128)(2,1)S(1)} %bitcast.34, bf16[2,3,64,128]{3,2,1,0:T(8,128)(2,1)S(1)} %pad.28.sp_ref, bf16[2,3,64,128]{3,2,1,0:T(8,128)(2,1)S(1)} %pad.29.oc_ref, bf16[432,16]{1,0:T(8,128)(2,1)S(1)} %bitcast.37, ...), custom_call_target="tpu_custom_call" | custom-call | tf_op jit(solution)/shard_map/pallas_call | solution.py:295
  45.6 0.8 %copy.48 = bf16[2,9,12,384]{3,0,1,2:T(2,128)(2,1)} copy(bf16[2,9,12,384]{3,2,1,0:T(8,128)(2,1)S(1)} %bitcast.38) | data formatting | bytes 331776
  46.4 0.2 reshape.49
  46.7 0.3 rev.27
  46.9 0.1 broadcast_multiply_fusion
  47.0 1.0 %copy.37 = f32[3,3,3,12,12]{4,3,2,1,0:T(8,128)} copy(f32[3,3,3,12,12]{3,2,1,0,4:T(4,128)S(1)} %broadcast_multiply_fusion) | data formatting | bytes 31104
  48.0 0.1 slice.28
  48.1 0.2 copy.39
  48.3 0.7 %reverse_multiply_fusion.1 = f32[3,3,60,12]{2,3,1,0:T(8,128)} fusion(f32[3,3,60,12]{2,3,1,0:T(8,128)S(1)} %copy.39), kind=kLoop, calls=%fused_computation.5 | loop fusion | flops 6480 | bytes 51840 | tf_op jit(solution)/shard_map/div | solution.py:334
  48.9 0.7 %reverse_multiply_fusion = f32[3,3,60,60]{3,2,1,0:T(8,128)} fusion(f32[3,3,60,60]{3,2,1,0:T(8,128)S(1)} %bitcast.39), kind=kLoop, calls=%fused_computation | loop fusion | flops 32400 | bytes 259200 | tf_op jit(solution)/shard_map/div | solution.py:334
  (17 shorter events, 0.4 us)
Async XLA Ops:
  2.3 0.9 %copy-start.6 = (bf16[60,2,3,128]{3,1,2,0:T(2,128)(2,1)S(1)}, bf16[60,2,3,128]{3,1,2,0:T(2,128)(2,1)}, u32[]{:S(2)}) copy-start(bf16[60,2,3,128]{3,1,2,0:T(2,128)(2,1)} %param.12) | copy-start | bytes 276484
  3.4 0.9 %copy-start.5 = (bf16[3,3,3,12,12]{4,3,2,1,0:T(8,128)(2,1)S(1)}, bf16[3,3,3,12,12]{4,3,2,1,0:T(8,128)(2,1)}, u32[]{:S(2)}) copy-start(bf16[3,3,3,12,12]{4,3,2,1,0:T(8,128)(2,1)} %param.13) | copy-start | bytes 23332
  4.3 0.9 %copy-start.4 = (bf16[3,3,60,60]{3,2,1,0:T(8,128)(2,1)S(1)}, bf16[3,3,60,60]{3,2,1,0:T(8,128)(2,1)}, u32[]{:S(2)}) copy-start(bf16[3,3,60,60]{3,2,1,0:T(8,128)(2,1)} %param.15) | copy-start | bytes 194404
  5.3 0.9 %copy-start.2 = (bf16[12,2,9,384]{3,1,2,0:T(2,128)(2,1)S(1)}, bf16[12,2,9,384]{3,1,2,0:T(2,128)(2,1)}, u32[]{:S(2)}) copy-start(bf16[12,2,9,384]{3,1,2,0:T(2,128)(2,1)} %param.9) | copy-start | bytes 497668
  6.2 0.9 %copy-start.3 = (bf16[12,2,9,384]{3,1,2,0:T(2,128)(2,1)S(1)}, bf16[12,2,9,384]{3,1,2,0:T(2,128)(2,1)}, u32[]{:S(2)}) copy-start(bf16[12,2,9,384]{3,1,2,0:T(2,128)(2,1)} %param.10) | copy-start | bytes 497668
  7.1 1.0 %copy-start.1 = (bf16[384,384]{1,0:T(8,128)(2,1)S(1)}, bf16[384,384]{1,0:T(8,128)(2,1)}, u32[]{:S(2)}) copy-start(bf16[384,384]{1,0:T(8,128)(2,1)} %constant.15.clone.pick_ref) | copy-start | bytes 884740
  7.2 1.0 %copy-start = (bf16[384,384]{1,0:T(8,128)(2,1)S(1)}, bf16[384,384]{1,0:T(8,128)(2,1)}, u32[]{:S(2)}) copy-start(bf16[384,384]{1,0:T(8,128)(2,1)} %constant.16.clone.back_ref) | copy-start | bytes 884740
where the time goes:
time: 50 us; the launch traced here: 49.7 us
  Pallas kernels  37.4 us (75%)
  local copies, waits for them, and re-layouts  10 us (20%)
  other arithmetic  1.45 us (3%)
  between operations  0.81 us (2%)
    pallas_call x1, Pallas kernels, on_device(): pl.pallas_call(functools.partial(kernel, ny, nz, rows), out_shape=(jax.Sh...  37.4 us
    unnamed x23, local copies, waits for them, and re-layouts  8.41 us

commit v1 on v0

v1 whole, which is shorter than its diff:
```python
import functools
import math

import jax
import jax.numpy as jnp
from jax import lax
from jax.experimental import pallas as pl
from jax.experimental.pallas import tpu as pltpu
from jax.sharding import PartitionSpec as P

MESH = pl.DeviceIdType.MESH
F32, BF16 = jnp.float32, jnp.bfloat16


def dot(a, b, da, db):
    return lax.dot_general(a, b, (((da,), (db,)), ((), ())), preferred_element_type=F32)


def neighbour_moves(sections):
    return [(z, y, s) for z in sections for y in (-1, 0, 1) for s in (0, 1) if (z, y, s) != (0, 0, 0)]


COARSE = neighbour_moves((0,))
FINE = neighbour_moves((-1, 0, 1))


class Sum:
    def __init__(self, ny, nz, source, inbox, part, line, total, sems):
        gy, gz, gx = lax.axis_index("gy"), lax.axis_index("gz"), lax.axis_index("gx")
        self.n, self.ny = 2 * nz, ny
        self.share = source.shape[0] // self.n
        self.source, self.inbox, self.part, self.line, self.total = source, inbox, part, line, total
        self.sems, self.me, self.gy = sems, gz * 2 + gx, gy
        self.mine = self.at(self.me)
        self.sent = []

    def at(self, member):
        return pl.ds(pl.multiple_of(member * self.share, 8), self.share)

    def copy(self, kind, j, src, dst, device):
        one = pltpu.make_async_remote_copy(
            src_ref=src, dst_ref=dst, send_sem=self.sems.at[2 * kind, j - 1],
            recv_sem=self.sems.at[2 * kind + 1, j - 1], device_id=device, device_id_type=MESH,
        )
        one.start()
        self.sent.append(one)
        return one

    def member(self, j):
        peer = lax.rem(self.me + j, self.n)
        return peer, {"gz": lax.div(peer, 2), "gx": lax.rem(peer, 2)}

    def scatter(self):
        self.copies = []
        for j in range(1, self.n):
            peer, device = self.member(j)
            self.copies.append(self.copy(0, j, self.source.at[self.at(peer)], self.inbox.at[j - 1], device))

    def exchange(self):
        for one in self.copies:
            one.wait_recv()
        total = self.source[self.mine]
        for j in range(self.n - 1):
            total = total + self.inbox[j]
        self.part[...] = total
        self.copies = [
            self.copy(1, j, self.part, self.line.at[j - 1], {"gy": lax.rem(self.gy + j, self.ny)})
            for j in range(1, self.ny)
        ]

    def gather(self):
        for one in self.copies:
            one.wait_recv()
        total = self.part[...]
        for j in range(self.ny - 1):
            total = total + self.line[j]
        self.total[self.mine] = total
        self.copies = [
            self.copy(2, j, self.total.at[self.mine], self.total.at[self.mine], self.member(j)[1])
            for j in range(1, self.n)
        ]

    def finish(self):
        for one in self.copies:
            one.wait_recv()


def kernel(
    ny, nz, scales,
    bi_ref, fp_ref, sp_ref, oc_ref, k1_ref, k2_ref, k3_ref,
    out_ref, first_ref, second_ref, third_ref,
    cot, delta, fine, col, ext, split, gather, k1, k2, k3, w1, w2, w3,
    sums1, sums2, sums3,
    cot_s, cot_r, delta_s, delta_r, fine_s, fine_r, load,
):
    gy, gz, gx = lax.axis_index("gy"), lax.axis_index("gz"), lax.axis_index("gx")

    def there(z, y):
        ok = None
        for at, step, size in ((gz, z, nz), (gy, y, ny)):
            if step:
                one = at < size - 1 if step > 0 else at > 0
                ok = one if ok is None else jnp.logical_and(ok, one)
        return ok

    def guarded(z, y, run):
        ok = there(z, y)
        if ok is None:
            run()
        else:
            pl.when(ok)(run)

    def device(z, y, s):
        return {"gz": gz + z, "gy": gy + y, "gx": 1 - gx if s else gx}

    loads = [
        pltpu.make_async_copy(src, dst, load.at[at])
        for at, (src, dst) in enumerate(((k1_ref, k1), (k2_ref, k2), (k3_ref, k3)))
    ]
    for one in loads:
        one.start()

    cot[...] = jnp.zeros_like(cot)
    delta[...] = jnp.zeros_like(delta)
    fine[...] = jnp.zeros_like(fine)
    for z in range(2):
        for y in range(3):
            cot[0, z, y + 1] = oc_ref[z, y]

    barrier = pltpu.get_barrier_semaphore()
    count = jnp.int32(0)
    for z, y, s in FINE:
        def greet(z=z, y=y, s=s):
            pl.semaphore_signal(barrier, inc=1, device_id=device(z, y, s), device_id_type=MESH)
        guarded(z, y, greet)
        ok = there(z, y)
        count = count + (1 if ok is None else ok.astype(jnp.int32))
    for j in range(1, 2 * nz):
        peer = lax.rem(gz * 2 + gx + j, 2 * nz)
        pl.semaphore_signal(
            barrier, inc=1, device_id={"gz": lax.div(peer, 2), "gx": lax.rem(peer, 2)}, device_id_type=MESH
        )
    for j in range(1, ny):
        pl.semaphore_signal(barrier, inc=1, device_id={"gy": lax.rem(gy + j, ny)}, device_id_type=MESH)
    pl.semaphore_wait(barrier, count + (2 * nz - 1) + (ny - 1))

    def halo_copy(buf, send, recv, moves, m, arriving=False):
        z, y, s = moves[m]
        zs = slice(0, 2) if buf.shape[1] == 2 else slice(1, 3)
        zd = zs
        if z:
            zs, zd = (slice(2, 3), slice(0, 1)) if z > 0 else (slice(1, 2), slice(3, 4))
        ys = yd = slice(1, 4)
        if y:
            ys, yd = (slice(3, 4), slice(0, 1)) if y > 0 else (slice(1, 2), slice(4, 5))
        return pltpu.make_async_remote_copy(
            src_ref=buf.at[0, zs, ys], dst_ref=buf.at[s, zd, yd],
            send_sem=send.at[m], recv_sem=recv.at[m],
            device_id=device(z, y, s), device_id_type=MESH,
        )

    def start_halo(buf, send, recv, moves):
        for m, (z, y, s) in enumerate(moves):
            guarded(z, y, lambda m=m: halo_copy(buf, send, recv, moves, m).start())

    def wait_halo(buf, send, recv, moves):
        for m, (z, y, s) in enumerate(moves):
            guarded(-z, -y, lambda m=m: halo_copy(buf, send, recv, moves, m).wait_recv())

    def wait_sent(buf, send, recv, moves):
        for m, (z, y, s) in enumerate(moves):
            guarded(z, y, lambda m=m: halo_copy(buf, send, recv, moves, m).wait_send())

    def shifted(own, other):
        own, other = own.astype(F32), other.astype(F32)
        lane = lax.broadcasted_iota(jnp.int32, own.shape, 1)
        left = jnp.where(gx == 1, other, 0.0)
        right = jnp.where(gx == 0, other, 0.0)
        before = pltpu.roll(jnp.where(lane == 127, left, own), 1, 1)
        after = pltpu.roll(jnp.where(lane == 0, right, own), 127, 1)
        return before, after

    def columns(buf):
        for z in range(2):
            for y in range(5):
                own = buf[0, z, y]
                before, after = shifted(own, buf[1, z, y])
                for ex, slab in enumerate((before.astype(BF16), own, after.astype(BF16))):
                    for ey in range(3):
                        yc = y - ey
                        if 0 <= yc < 3:
                            r = (ey * 3 + ex) * 64
                            c = (z * 3 + yc) * 128
                            col[r:r + 64, c:c + 128] = slab

    start_halo(cot, cot_s, cot_r, COARSE)

    row = lax.broadcasted_iota(jnp.int32, (384, 384), 0)
    lane = lax.broadcasted_iota(jnp.int32, (384, 384), 1)
    pick = jnp.where(row == (lane & 127) * 3 + (lane >> 7), 1.0, 0.0).astype(BF16)
    split[...] = dot(fp_ref[...], pick, 1, 0)

    def phase(z, a, b):
        return jnp.concatenate(
            [split[(z * 9 + 3 * yc + a) * 16:(z * 9 + 3 * yc + a) * 16 + 16, b * 128:b * 128 + 128] for yc in range(3)],
            axis=1,
        )

    pooled = []
    for z in range(2):
        window = [jnp.maximum(phase(z, k // 3, k % 3), 0.0) for k in range(9)]
        top = functools.reduce(jnp.maximum, window)
        first = jnp.full(top.shape, 9.0, F32)
        for k in reversed(range(9)):
            first = jnp.where(window[k] == top, float(k), first)
        first = jnp.where(top > 0.0, first, 9.0).astype(BF16)
        for y in range(3):
            fine[0, z + 1, y + 1, 16:32] = first[:, y * 128:y * 128 + 128]
        pooled.append(top.astype(BF16))
    pooled = jnp.concatenate(pooled, axis=1)
    second_relu = jnp.concatenate(
        [jnp.maximum(sp_ref[z, y], jnp.zeros((), BF16)) for z in range(2) for y in range(3)], axis=1
    )
    split[...] = dot(bi_ref[...], pick, 1, 0)

    for one in loads:
        one.wait()
    for w in (w1, w2, w3):
        w[...] = jnp.zeros_like(w)
    unit = jnp.where(
        lax.broadcasted_iota(jnp.int32, (12, 16), 0) == lax.broadcasted_iota(jnp.int32, (12, 16), 1), 1.0, 0.0
    ).astype(BF16)
    for ey in range(3):
        for ex in range(3):
            e = ey * 3 + ex
            w3[e * 64:e * 64 + 60, 0:60] = k3[2 - ey, 2 - ex].astype(F32)
            w2[e * 64:e * 64 + 60] = dot(k2[2 - ey, 2 - ex], unit, 0, 0)
            for ez in range(3):
                r = (ez * 9 + e) * 16
                w1[r:r + 12, 0:12] = k1[2 - ez, 2 - ey, 2 - ex].astype(F32)

    first_sum, second_sum, third_sum = (Sum(ny, nz, *refs) for refs in (sums1, sums2, sums3))
    for one in (first_sum, second_sum, third_sum):
        one.source[...] = jnp.zeros_like(one.source)

    def put(one, value):
        tall, wide = value.shape
        for t in range(-(-wide // 128)):
            part = value[:, t * 128:min(wide, t * 128 + 128)]
            one.source[t * tall:t * tall + tall, 0:part.shape[1]] = part

    def tap(one, tall, e, depth):
        at = e * depth
        block = one.total[at // 128 * tall:at // 128 * tall + tall]
        return block[:, at % 128:at % 128 + depth]

    wait_halo(cot, cot_s, cot_r, COARSE)
    columns(cot)
    third_back = dot(w3[...].astype(BF16), col[...], 0, 0)
    for z in range(2):
        for y in range(3):
            c = (z * 3 + y) * 128
            delta[0, z, y + 1] = jnp.where(
                sp_ref[z, y].astype(F32) > 0.0, third_back[:, c:c + 128], 0.0
            ).astype(BF16)
    start_halo(delta, delta_s, delta_r, COARSE)
    put(third_sum, dot(second_relu, col[...], 1, 1))
    third_sum.scatter()
    wait_halo(delta, delta_s, delta_r, COARSE)
    columns(delta)
    pooled_back = dot(w2[...].astype(BF16), col[...], 0, 0).astype(BF16)
    for z in range(2):
        for y in range(3):
            c = (z * 3 + y) * 128
            fine[0, z + 1, y + 1, 0:16] = pooled_back[:, c:c + 128]
    start_halo(fine, fine_s, fine_r, FINE)
    third_sum.exchange()
    put(second_sum, dot(pooled, col[...], 1, 1))
    second_sum.scatter()
    wait_halo(fine, fine_s, fine_r, FINE)
    third_sum.gather()

    for z in range(4):
        own = fine[0, z].reshape(160, 128)
        before, after = shifted(own, fine[1, z].reshape(160, 128))
        own = own.astype(F32)
        views = []
        for src in (before, own, after):
            value = [src[y * 32:y * 32 + 16] for y in range(5)]
            place = [src[y * 32 + 16:y * 32 + 32] for y in range(5)]
            views.append((value, place))
        for ea in range(5):
            a, up = ((2, 0), (0, 1), (1, 1), (2, 1), (0, 2))[ea]
            for eb in range(5):
                b, side = ((2, 0), (0, 1), (1, 1), (2, 1), (0, 2))[eb]
                value, place = views[side]
                for yc in range(3):
                    block = jnp.where(place[yc + up] == float(a * 3 + b), value[yc + up], 0.0)
                    r = (ea * 5 + eb) * 16
                    ext[z, r:r + 16, yc * 128:yc * 128 + 128] = block.astype(BF16)

    second_sum.exchange()

    def stack(z, a, b):
        return jnp.concatenate(
            [
                ext[z + ez, ((a + ey) * 5 + b) * 16:((a + ey) * 5 + b) * 16 + 48]
                for ez in range(3) for ey in range(3)
            ],
            axis=0,
        )

    places = [(a, b) for a in range(3) for b in range(3)]
    first = jnp.zeros((16, 432), F32)
    for z in range(2):
        for a, b in places:
            first = first + dot(phase(z, a, b).astype(BF16), stack(z, a, b), 1, 1)
    put(first_sum, first)
    first_sum.scatter()
    second_sum.gather()
    weights = w1[...].astype(BF16)
    for z in range(2):
        for a, b in places:
            back = dot(weights, stack(z, a, b), 0, 0).astype(BF16)
            for yc in range(3):
                r = (z * 9 + 3 * yc + a) * 16
                gather[r:r + 16, b * 128:b * 128 + 128] = back[:, yc * 128:yc * 128 + 128]
        if z == 0:
            first_sum.exchange()
    first_sum.gather()
    out_ref[...] = dot(gather[...], pick, 1, 1).astype(BF16)
    first_scale, second_scale, third_scale = scales
    third_sum.finish()
    second_sum.finish()
    for ey in range(3):
        for ex in range(3):
            e = ey * 3 + ex
            second_ref[2 - ey, 2 - ex] = tap(second_sum, 16, e, 64)[0:12, 0:60] * second_scale
    for t in range(5):
        block = third_sum.total[t * 64:t * 64 + 64].T
        for e in range(2 * t, min(2 * t + 2, 9)):
            r = (e - 2 * t) * 64
            third_ref[2 - e // 3, 2 - e % 3] = block[r:r + 60, 0:60] * third_scale
    first_sum.finish()
    for t in range(4):
        block = first_sum.total[t * 16:t * 16 + 16].T
        for e in range(8 * t, min(8 * t + 8, 27)):
            r = (e - 8 * t) * 16
            first_ref[2 - e // 9, 2 - e // 3 % 3, 2 - e % 3] = block[r:r + 12, 0:12] * first_scale
    for one in (first_sum, second_sum, third_sum):
        for copy in one.sent:
            copy.wait_send()
    wait_sent(cot, cot_s, cot_r, COARSE)
    wait_sent(delta, delta_s, delta_r, COARSE)
    wait_sent(fine, fine_s, fine_r, FINE)


def on_device(
    block_input, first_pre, second_pre, output_cotangent, first_kernel, second_kernel, third_kernel
):
    ny, nz, nx = (lax.axis_size(axis) for axis in ("gy", "gz", "gx"))
    assert nx == 2 and block_input.shape == (12, 2, 9, 384)
    devices = ny * nz * nx
    voxels = 2 * 9 * 384 * devices
    coarse_scale = 1.0 / math.sqrt(voxels // 9)
    fine_scale = 1.0 / math.sqrt(voxels)

    def fine_rows(x):
        return jnp.pad(x.transpose(1, 2, 0, 3), ((0, 0), (0, 0), (0, 4), (0, 0))).reshape(288, 384)

    def coarse_rows(x):
        return jnp.pad(x.transpose(1, 2, 0, 3), ((0, 0), (0, 0), (0, 4), (0, 0)))

    dma = pltpu.SemaphoreType.DMA
    vmem = pl.BlockSpec(memory_space=pltpu.VMEM)
    slots = max(2 * nz, ny)

    def sums(rows):
        rows = -(-rows // (16 * nz)) * 16 * nz
        share = rows // (2 * nz)
        return (
            pltpu.VMEM((rows, 128), F32), pltpu.VMEM((2 * nz - 1, share, 128), F32), pltpu.VMEM((share, 128), F32),
            pltpu.VMEM((ny - 1, share, 128), F32), pltpu.VMEM((rows, 128), F32), dma((6, slots)),
        )

    out, first, second, third = pl.pallas_call(
        functools.partial(kernel, ny, nz, (fine_scale, coarse_scale, coarse_scale)),
        out_shape=(
            jax.ShapeDtypeStruct((288, 384), BF16),
            jax.ShapeDtypeStruct((3, 3, 3, 12, 12), F32),
            jax.ShapeDtypeStruct((3, 3, 12, 60), F32),
            jax.ShapeDtypeStruct((3, 3, 60, 60), F32),
        ),
        in_specs=[vmem] * 4 + [pl.BlockSpec(memory_space=pltpu.HBM)] * 3,
        out_specs=(vmem,) * 4,
        scratch_shapes=[
            pltpu.VMEM((2, 2, 5, 64, 128), BF16),
            pltpu.VMEM((2, 2, 5, 64, 128), BF16),
            pltpu.VMEM((2, 4, 5, 32, 128), BF16),
            pltpu.VMEM((576, 768), BF16),
            pltpu.VMEM((4, 400, 384), BF16),
            pltpu.VMEM((288, 384), F32),
            pltpu.VMEM((288, 384), BF16),
            pltpu.VMEM((3, 3, 3, 12, 12), BF16),
            pltpu.VMEM((3, 3, 12, 60), BF16),
            pltpu.VMEM((3, 3, 60, 60), BF16),
            pltpu.VMEM((432, 16), F32),
            pltpu.VMEM((576, 16), F32),
            pltpu.VMEM((576, 64), F32),
            sums(64), sums(80), sums(320),
            dma((len(COARSE),)), dma((len(COARSE),)),
            dma((len(COARSE),)), dma((len(COARSE),)),
            dma((len(FINE),)), dma((len(FINE),)),
            dma((3,)),
        ],
        compiler_params=pltpu.CompilerParams(
            collective_id=0, has_side_effects=True, vmem_limit_bytes=48 * 1024 * 1024
        ),
    )(
        fine_rows(block_input), fine_rows(first_pre), coarse_rows(second_pre), coarse_rows(output_cotangent),
        first_kernel, second_kernel.transpose(0, 1, 3, 2), third_kernel,
    )
    block_gradient = out.reshape(2, 9, 16, 384)[:, :, :12].transpose(2, 0, 1, 3)
    return block_gradient, first, second.transpose(0, 1, 3, 2), third


def solution(mesh):
    volume = P(None, "gz", ("groups", "gy"), "gx")
    return jax.shard_map(
        on_device,
        mesh=mesh,
        in_specs=(volume,) * 4 + (P(),) * 3,
        out_specs=(
            volume,
            P("groups", None, None, None, None),
            P("groups", None, None, None),
            P("groups", None, None, None),
        ),
        check_vma=False,
    )
```

time: 50 us -> 40.5 us (0.81)
  Pallas kernels: 37.4 us -> 32.1 us
  local copies, waits for them, and re-layouts: 10 us -> 7.42 us
  other arithmetic: 1.45 us -> 0 us
    pallas_call x1, Pallas kernels: 37.4 us -> 32.1 us  [on_device(): pl.pallas_call(functools.partial(kernel, ny, nz, (fine_scale, coarse_scal...]
    div x3 -> x0, other arithmetic: 1.45 us -> none  [the longest x1 0.74 us: on_device(): third / coarse_scale]
    unnamed x23 -> x20, local copies, waits for them, and re-layouts: 8.41 us -> 7.34 us
    rev x4 -> x0, local copies, waits for them, and re-layouts: 1.04 us -> none  [the longest x1 0.77 us: on_device(): jnp.flip(second_kernel, (0, 1))]
where the time goes in v1:
time: 40.5 us; the launch traced here: 40.3 us
  Pallas kernels  32.1 us (79%)
  local copies, waits for them, and re-layouts  7.42 us (18%)
  between operations  0.73 us (2%)
    pallas_call x1, Pallas kernels, on_device(): pl.pallas_call(functools.partial(kernel, ny, nz, (fine_scale, coarse_scal...  32.1 us
    unnamed x20, local copies, waits for them, and re-layouts  7.34 us

profile of v1, /device:TPU:0, one launch (start us, length us, event | category | flops | bytes accessed | tf_op | source)
XLA Modules:
  0.0 40.3 jit_solution(897675810767321730)
XLA Ops:
  0.6 0.9 %copy.24 = bf16[60,2,3,128]{3,0,2,1:T(8,128)(2,1)S(1)} copy(bf16[60,2,3,128]{3,1,2,0:T(2,128)(2,1)} %param.9) | data formatting | bytes 184320 | tf_op args[2]
  1.5 0.0 copy-start.5
  1.6 0.9 %copy-done.5 = bf16[60,2,3,128]{3,1,2,0:T(2,128)(2,1)S(1)} copy-done((bf16[60,2,3,128]{3,1,2,0:T(2,128)(2,1)S(1)}, bf16[60,2,3,128]{3,1,2,0:T(2,128)(2,1)}, u32[]{:S(2)}) %copy-start.5) | copy-done | bytes 92184
  2.4 0.0 copy-start.3
  2.5 0.9 %copy-done.3 = bf16[12,2,9,384]{3,1,2,0:T(2,128)(2,1)S(1)} copy-done((bf16[12,2,9,384]{3,1,2,0:T(2,128)(2,1)S(1)}, bf16[12,2,9,384]{3,1,2,0:T(2,128)(2,1)}, u32[]{:S(2)}) %copy-start.3) | copy-done | bytes 165912
  3.4 0.0 copy-start.4
  3.4 0.9 %copy-done.4 = bf16[12,2,9,384]{3,1,2,0:T(2,128)(2,1)S(1)} copy-done((bf16[12,2,9,384]{3,1,2,0:T(2,128)(2,1)S(1)}, bf16[12,2,9,384]{3,1,2,0:T(2,128)(2,1)}, u32[]{:S(2)}) %copy-start.4) | copy-done | bytes 165912
  4.3 0.0 copy-start
  4.3 0.0 copy-start.1
  4.4 0.0 copy-start.2
  4.4 0.8 %copy-done = bf16[3,3,60,60]{3,2,1,0:T(8,128)(2,1)S(1)} copy-done((bf16[3,3,60,60]{3,2,1,0:T(8,128)(2,1)S(1)}, bf16[3,3,60,60]{3,2,1,0:T(8,128)(2,1)}, u32[]{:S(2)}) %copy-start) | copy-done | bytes 64824
  5.2 0.1 copy-done.1
  5.3 0.0 copy-done.2
  5.3 32.1 %shard_map.102 = (bf16[288,384]{1,0:T(8,128)(2,1)S(1)}, f32[3,3,3,12,12]{4,3,2,1,0:T(8,128)S(1)}, f32[3,3,12,60]{3,2,1,0:T(8,128)S(1)}, f32[3,3,60,60]{3,2,1,0:T(8,128)S(1)}) custom-call(bf16[288,384]{1,0:T(8,128)(2,1)S(1)} %bitcast.17, bf16[288,384]{1,0:T(8,128)(2,1)S(1)} %bitcast.18, bf16[2,3,64,128]{3,2,1,0:T(8,128)(2,1)S(1)} %pad.16.sp_ref, ...), custom_call_target="tpu_custom_call" | custom-call | tf_op jit(solution)/shard_map/pallas_call | solution.py:386
  37.4 0.8 %copy.22 = bf16[2,9,12,384]{3,0,1,2:T(2,128)(2,1)} copy(bf16[2,9,12,384]{3,2,1,0:T(8,128)(2,1)S(1)} %bitcast.19) | data formatting | bytes 331776
  38.2 0.7 %copy.28 = f32[3,3,3,12,12]{4,3,2,1,0:T(8,128)} copy(f32[3,3,3,12,12]{4,3,2,1,0:T(8,128)S(1)} %get-tuple-element.17) | data formatting | bytes 31104
  38.9 0.6 %copy.29 = f32[3,3,60,12]{2,3,1,0:T(8,128)} copy(f32[3,3,60,12]{2,3,1,0:T(8,128)S(1)} %bitcast.20) | data formatting | bytes 51840
  39.6 0.7 %copy.30 = f32[3,3,60,60]{3,2,1,0:T(8,128)} copy(f32[3,3,60,60]{3,2,1,0:T(8,128)S(1)} %get-tuple-element.19) | data formatting | bytes 259200
  (7 shorter events, 0.2 us)
Async XLA Ops:
  1.5 0.9 %copy-start.5 = (bf16[60,2,3,128]{3,1,2,0:T(2,128)(2,1)S(1)}, bf16[60,2,3,128]{3,1,2,0:T(2,128)(2,1)}, u32[]{:S(2)}) copy-start(bf16[60,2,3,128]{3,1,2,0:T(2,128)(2,1)} %param.10) | copy-start | bytes 276484
  2.4 0.9 %copy-start.3 = (bf16[12,2,9,384]{3,1,2,0:T(2,128)(2,1)S(1)}, bf16[12,2,9,384]{3,1,2,0:T(2,128)(2,1)}, u32[]{:S(2)}) copy-start(bf16[12,2,9,384]{3,1,2,0:T(2,128)(2,1)} %param.7) | copy-start | bytes 497668
  3.4 0.9 %copy-start.4 = (bf16[12,2,9,384]{3,1,2,0:T(2,128)(2,1)S(1)}, bf16[12,2,9,384]{3,1,2,0:T(2,128)(2,1)}, u32[]{:S(2)}) copy-start(bf16[12,2,9,384]{3,1,2,0:T(2,128)(2,1)} %param.8) | copy-start | bytes 497668
  4.3 0.9 %copy-start = (bf16[3,3,60,60]{3,2,1,0:T(8,128)(2,1)S(1)}, bf16[3,3,60,60]{3,2,1,0:T(8,128)(2,1)}, u32[]{:S(2)}) copy-start(bf16[3,3,60,60]{3,2,1,0:T(8,128)(2,1)} %k3_ref.1) | copy-start | bytes 194404
  4.3 1.0 %copy-start.1 = (bf16[3,3,3,12,12]{4,3,2,1,0:T(8,128)(2,1)S(1)}, bf16[3,3,3,12,12]{4,3,2,1,0:T(8,128)(2,1)}, u32[]{:S(2)}) copy-start(bf16[3,3,3,12,12]{4,3,2,1,0:T(8,128)(2,1)} %k1_ref.1) | copy-start | bytes 23332
  4.4 1.0 %copy-start.2 = (bf16[3,3,60,12]{2,3,1,0:T(8,128)(2,1)S(1)}, bf16[3,3,60,12]{2,3,1,0:T(8,128)(2,1)}, u32[]{:S(2)}) copy-start(bf16[3,3,60,12]{2,3,1,0:T(8,128)(2,1)} %param.12) | copy-start | bytes 38884
